TPU v7x, 32 devices: a whole 2x2x4 slice. The times are simulated.
32 devices in a mesh: tm: 8 (over y, x, core), tile: 4 (over z).
Axes of the slice: x: 2, y: 2, z: 4, core: 2. Of those that a mesh axis runs over, the one named last changes fastest.
Arguments:
- velocity_u: float32 [384, 2, 16, 1024], P('tm', None, None, 'tile'), may hold values from -12 to 12
- velocity_v: float32 [384, 2, 16, 1024], P('tm', None, None, 'tile'), may hold values from -12 to 12
- land_sea: int32 [16, 1024], P(None, 'tile'), may hold values 0 or 1
- bottom_level: int32 [16, 1024], P(None, 'tile'), may hold values from 0 to 2
- spacing_x: float32 [16, 1024], P(None, 'tile'), may hold values from 0.5 to 2
- spacing_y: float32 [16, 1024], P(None, 'tile'), may hold values from 0.5 to 2
Outputs:
- conversion_maps: bfloat16 [384, 2, 16, 1024], P('tm', None, None, 'tile')
- mean_map: float32 [2, 16, 1024], P(None, None, 'tile')
All inputs are finite; a program needn't handle non-finite values. No bound on the sum of `land_sea` on one device may be relied on, other than what follows from the above.
Results may differ from a plain program's by a relative error of at most 0.001.
Values sent between devices are 32-bit elements; how exact they have to be, the bound alone decides.
A program may use at most 64 MiB of HBM per device.

v0:
```python
import jax
import jax.numpy as jnp
from jax import lax
from jax.sharding import PartitionSpec as P

HALF = 24
SNAPS = 48
cutoff_freq = 1.0 / 40.0


def extended(x, sides, width):
    for axis, dim in sides:
        size, length = (lax.axis_size(axis), x.shape[dim])
        up = [(i, (i + 1) % size) for i in range(size - 1)]
        down = [(j, i) for i, j in up]
        last = lax.slice_in_dim(x, length - width, length, axis=dim)
        first = lax.slice_in_dim(x, 0, width, axis=dim)
        before = lax.ppermute(last, axis, up)
        after = lax.ppermute(first, axis, down)
        x = jnp.concatenate([before, x, after], axis=dim)
    return x


def band_matrix(count):
    out_rows = jnp.arange(count, dtype=jnp.int32)[:, None]
    in_cols = jnp.arange(count + 2 * HALF, dtype=jnp.int32)[None, :]
    offset = (in_cols - out_rows - HALF).astype(jnp.float32)
    weights = 2.0 * cutoff_freq * jnp.sinc(2.0 * cutoff_freq * offset) * jnp.sinc(offset / HALF)
    return jnp.where(jnp.abs(offset) <= HALF, weights, jnp.zeros_like(weights))


def lowpass(padded, validity, blocks, block):
    matrix = band_matrix(block)

    def one_block(block_id):
        start = block_id * block
        window = lax.dynamic_slice_in_dim(padded, start, block + 2 * HALF, 0)
        valid_part = lax.dynamic_slice_in_dim(validity, start, block + 2 * HALF, 0)
        weighted = jnp.dot(
            matrix, window, precision=lax.Precision.HIGHEST, preferred_element_type=jnp.float32
        )
        weight_sum = jnp.dot(
            matrix, valid_part, precision=lax.Precision.HIGHEST, preferred_element_type=jnp.float32
        )
        return weighted / weight_sum[:, None]

    result = lax.map(one_block, jnp.arange(blocks, dtype=jnp.int32))
    return result.reshape(blocks * block, padded.shape[1])


def wet_cells(land_sea, bottom_level, levels):
    level_ids = jnp.arange(levels, dtype=jnp.int32)[:, None, None]
    return ((land_sea[None] == 1) & (level_ids < bottom_level[None])).astype(jnp.float32)


def filter_series(series):
    length = series.shape[0]
    flattened = series.reshape(length, -1)
    padded = jnp.pad(flattened, ((HALF, HALF), (0, 0)))
    validity = jnp.pad(jnp.ones((length,), jnp.float32), (HALF, HALF))
    return lowpass(padded, validity, length // SNAPS, SNAPS).reshape(series.shape)


def shards(velocity_u, velocity_v, land_sea, bottom_level, spacing_x, spacing_y):
    block_len = velocity_u.shape[0]
    total_len = block_len * lax.axis_size("tm")
    stacked = jnp.stack([velocity_u, velocity_v], axis=1)
    full_shape = stacked.shape
    flat_cells = stacked.reshape(block_len, 2, -1)
    series_mean = filter_series(
        lax.all_to_all(flat_cells, "tm", split_axis=2, concat_axis=0, tiled=True)
    )
    mean_flat = lax.all_to_all(series_mean, "tm", split_axis=0, concat_axis=2, tiled=True)
    mean_flow = mean_flat.reshape(full_shape)
    eddies = stacked - mean_flow
    wet_mask = wet_cells(land_sea, bottom_level, full_shape[2])
    masked = mean_flow * wet_mask[None, None]
    edge_cols = jnp.concatenate([masked[..., :1], masked[..., -1:]], axis=4)
    edge_ext = extended(edge_cols, (("tile", 4),), 1)
    left_col = edge_ext[..., :1]
    right_col = edge_ext[..., 3:4]
    ahead = jnp.concatenate([masked[..., 1:], right_col], axis=4)
    behind = jnp.concatenate([left_col, masked[..., :-1]], axis=4)
    grad_x = (ahead - behind) * (0.5 / spacing_x)
    row_padded = jnp.pad(masked, ((0, 0), (0, 0), (0, 0), (1, 1), (0, 0)))
    grad_y = (row_padded[..., 2:, :] - row_padded[..., :-2, :]) * (0.5 / spacing_y)
    eddy_u = eddies[:, 0]
    eddy_v = eddies[:, 1]
    total = (
        eddy_u * eddy_u * grad_x[:, 0]
        + eddy_u * eddy_v * (grad_y[:, 0] + grad_x[:, 1])
        + eddy_v * eddy_v * grad_y[:, 1]
    )
    conversion = -wet_mask[None] * total
    summed = lax.psum(jnp.sum(conversion, axis=0), "tm")
    return (conversion.astype(jnp.bfloat16), summed / total_len)


def solution(mesh):
    in_specs = (
        P("tm", None, None, "tile"),
        P("tm", None, None, "tile"),
        P(None, "tile"),
        P(None, "tile"),
        P(None, "tile"),
        P(None, "tile"),
    )
    out_specs = (P("tm", None, None, "tile"), P(None, None, "tile"))
    return jax.shard_map(shards, mesh=mesh, in_specs=in_specs, out_specs=out_specs, check_vma=False)
```

profile of v0, /device:TPU:0, one launch (start us, length us, event | category | flops | bytes accessed | tf_op | source)
XLA Modules:
  0.0 262.7 jit_solution(6098952019784487532)
XLA Ops:
  0.6 0.0 copy-start.3
  0.6 2.7 %stack.18 = f32[48,1,8192]{2,0,1:T(8,128)} reshape(f32[48,2,16,256]{3,2,1,0:T(8,128)} %param.9) | data formatting | bytes 3145728 | tf_op jit(solution)/shard_map/stack | solution.py:67
  3.3 1.4 stack.19
  4.8 2.1 pad_maximum_fusion
  6.9 8.0 %copy.21 = f32[48,2,8192]{0,1,2:T(2,128)} copy(f32[48,2,8192]{2,0,1:T(8,128)S(1)} %pad_maximum_fusion) | data formatting | bytes 6291456 | tf_op jit(solution)/shard_map/stack | solution.py:67
  14.9 16.2 %reshape.50 = f32[8,1,98304]{2,1,0:T(1,128)} reshape(f32[8192,2,48]{2,1,0:T(2,128)} %bitcast.49) | data formatting | bytes 6291456
  31.0 5.4 %all-to-all-start = ((f32[8,1,98304]{2,1,0:T(1,128)}), f32[8,1,98304]{2,1,0:T(1,128)S(1)}, u32[]{:S(2)}, u32[]{:S(2)}) async-start(f32[8,1,98304]{2,1,0:T(1,128)} %reshape.50), calls=%async_computation | async-start | bytes 6291456 | tf_op jit(solution)/shard_map/all_to_all | solution.py:71
  36.5 0.1 pad.13
  36.6 0.7 fusion.42
  37.2 36.8 %all-to-all-done = f32[8,1,98304]{2,1,0:T(1,128)S(1)} async-done(((f32[8,1,98304]{2,1,0:T(1,128)}), f32[8,1,98304]{2,1,0:T(1,128)S(1)}, u32[]{:S(2)}, u32[]{:S(2)}) %all-to-all-start) | async-done | bytes 3145760 | tf_op jit(solution)/shard_map/all_to_all | solution.py:71
  74.1 0.5 broadcast.65
  74.6 11.2 %reduce = f32[8,98304]{1,0:T(8,128)} reduce(f32[8,1,98304]{2,1,0:T(1,128)S(1)} %all-to-all-done, f32[]{:T(128)} %broadcast.65), dimensions={1}, to_apply=%all_to_all.22.reduce_sub_computation | reduce | bytes 6291460 | tf_op jit(solution)/shard_map/all_to_all | solution.py:71
  85.8 19.3 %reshape.51 = f32[8192,2,48]{2,1,0:T(2,128)} reshape(f32[8,98304]{1,0:T(8,128)} %reduce) | data formatting | bytes 6291456
  105.1 7.0 %copy.30 = f32[48,2,8,1024]{3,2,0,1:T(8,128)S(1)} copy(f32[48,2,8,1024]{0,1,3,2:T(2,128)} %bitcast.50) | data formatting | bytes 6291456 | tf_op jit(solution)/shard_map/all_to_all | solution.py:71
  112.1 2.4 copy.23
  114.5 1.4 copy.31
  115.9 0.4 pad.12
  116.3 34.3 %while.11 = (s32[]{:T(128)}, f32[8,48,2048]{2,1,0:T(8,128)}, s32[8]{0:T(128)S(1)}, f32[432,2048]{1,0:T(8,128)S(1)}, f32[48,96]{1,0:T(8,128)}, /*index=5*/f32[432...) while((s32[]{:T(128)}, f32[8,48,2048]{2,1,0:T(8,128)}, s32[8]{0:T(128)S(1)}, ...), condition=%wide.region_1.3_spmd.clone, body=%wide.region_0.2_spmd.clone.sunk | while | flops 113399816 | bytes 1224551 | solution.py:47
  116.4 0.6 dynamic_slice.24
  117.6 0.9 convolution_bitcast_fusion.2
  118.5 2.1 fusion.59
  120.7 0.6 dynamic_slice.24
  121.9 0.9 convolution_bitcast_fusion.2
  122.9 2.1 fusion.59
  125.0 0.6 dynamic_slice.24
  126.2 0.9 convolution_bitcast_fusion.2
  127.1 2.1 fusion.59
  129.2 0.6 dynamic_slice.24
  130.5 0.9 convolution_bitcast_fusion.2
  131.4 2.1 fusion.59
  133.5 0.6 dynamic_slice.24
  134.8 0.9 convolution_bitcast_fusion.2
  135.7 2.1 fusion.59
  137.8 0.6 dynamic_slice.24
  139.0 0.9 convolution_bitcast_fusion.2
  140.0 2.1 fusion.59
  142.1 0.6 dynamic_slice.24
  143.3 0.9 convolution_bitcast_fusion.2
  144.3 2.1 fusion.59
  146.4 0.6 dynamic_slice.24
  147.6 0.9 convolution_bitcast_fusion.2
  148.5 2.1 fusion.59
  150.6 5.6 %reshape_reshape.3 = f32[384,2,1024]{2,1,0:T(2,128)} reshape(f32[8,48,2048]{2,1,0:T(8,128)} %get-tuple-element.38) | data formatting | bytes 6291456 | tf_op jit(solution)/shard_map/reshape;reshape | solution.py:61
  156.2 4.0 %all-to-all-start.1 = ((f32[384,2,1024]{2,1,0:T(2,128)}), f32[384,2,1024]{2,1,0:T(2,128)S(1)}, u32[]{:S(2)}, u32[]{:S(2)}) async-start(f32[384,2,1024]{2,1,0:T(2,128)} %reshape_reshape.3), calls=%async_computation.1 | async-start | bytes 6291456 | tf_op jit(solution)/shard_map/all_to_all | solution.py:73
  160.3 37.7 %all-to-all-done.1 = f32[384,2,1024]{2,1,0:T(2,128)S(1)} async-done(((f32[384,2,1024]{2,1,0:T(2,128)}), f32[384,2,1024]{2,1,0:T(2,128)S(1)}, u32[]{:S(2)}, u32[]{:S(2)}) %all-to-all-start.1) | async-done | bytes 3145760 | tf_op jit(solution)/shard_map/all_to_all | solution.py:73
  198.0 1.0 copy.24
  199.0 1.8 copy.25
  200.8 2.6 reshape.47
  203.4 5.7 %maximum_subtract_fusion = (f32[48,2,2,16,256]{4,3,2,1,0:T(8,128)}, f32[48,2,2,16,256]{4,3,2,1,0:T(8,128)S(1)}) fusion(f32[48,2,2,16,256]{4,3,2,1,0:T(8,128)} %reshape.47, f32[48,1,2,16,256]{4,3,2,1,0:T(8,128)} %bitcast.55, f32[48,1,2,16,256]{4,3,2,1,0:T(8,128)} %bitcast.56, f32[2,16,256]{2,1,0:T(8,128)S(1)} %fusion.15), kind=kLoop, calls=%fused_computation.12 | loop fusion | flops 2359296 | bytes 12615680 | tf_op jit(solution)/shard_map/sub | solution.py:75
  209.1 3.7 %fusion.47 = (f32[48,2,2,16,255]{4,3,2,1,0:T(8,128)}, f32[48,2,2,16,255]{4,3,2,1,0:T(8,128)}) fusion(f32[48,2,2,16,256]{4,3,2,1,0:T(8,128)S(1)} %get-tuple-element.70), kind=kLoop, calls=%fused_computation.85 | loop fusion | bytes 12533760 | tf_op jit(solution)/shard_map/slice | solution.py:83
  212.8 2.3 fusion.46
  215.1 2.2 copy.26
  217.3 1.3 collective-permute-start
  218.6 2.2 copy.28
  220.8 4.7 %collective-permute-start.1 = (f32[48,2,2,16,1]{0,3,4,2,1:T(8,128)S(1)}, f32[48,2,2,16,1]{0,3,4,2,1:T(8,128)S(1)}, u32[]{:S(2)}, u32[]{:S(2)}) collective-permute-start(f32[48,2,2,16,1]{0,3,4,2,1:T(8,128)S(1)} %copy.28), channel_id=1, source_target_pairs={{0,1},{1,2},{2,3},{4,5},{5,6},{6,7},{8,9},{9,10},{10,11},{12,13},{... | collective-permute-start | bytes 36872 | tf_op jit(solution)/shard_map/ppermute | solution.py:18
  225.5 2.4 fusion.7
  228.0 2.4 copy.27
  230.3 0.0 collective-permute-done.1
  230.3 2.4 copy.29
  232.7 4.3 %fusion.8 = f32[48,2,2,16,256]{4,3,2,1,0:T(8,128)S(1)} fusion(f32[48,2,2,16,1]{4,3,2,1,0:T(8,128)} %copy.27, f32[48,2,2,16,255]{4,3,2,1,0:T(8,128)} %get-tuple-element.74, f32[48,2,2,16,255]{4,3,2,1,0:T(8,128)S(1)} %copy-done.2, f32[48,2,2,16,1]{4,3,2,1,0:T(8,128)} %copy.29, f32[16,256]{1,0:T(8,128)S(1)} %broadcast_divide_fusion.1), kind=kLoop, calls=%fused_computation.15 | loop fusion | flops 3145728 | bytes 9453568 | tf_op jit(solution)/shard_map/mul | solution.py:84
  237.0 0.4 copy-done.1
  237.4 2.1 fusion.44
  239.5 22.3 %psum.7 = f32[2,16,256]{2,1,0:T(8,128)S(1)} all-reduce(f32[2,16,256]{2,1,0:T(8,128)S(1)} %get-tuple-element.67), channel_id=1, replica_groups=mesh['tm'=8,'tile'=4] {'tm'}, use_global_device_ids=true, to_apply=%region_3.5 | all-reduce | flops 8192 | bytes 65536 | tf_op jit(solution)/shard_map/psum | solution.py:95
  261.9 0.6 broadcast_multiply_fusion.1
  (23 shorter events, 0.1 us)
Async XLA Ops:
  0.6 2.7 %copy-start.3 = (f32[48,2,16,256]{3,2,1,0:T(8,128)S(1)}, f32[48,2,16,256]{3,2,1,0:T(8,128)}, u32[]{:S(2)}) copy-start(f32[48,2,16,256]{3,2,1,0:T(8,128)} %param.10) | copy-start | bytes 4718596
  31.0 43.1 %all-to-all-start = ((f32[8,1,98304]{2,1,0:T(1,128)}), f32[8,1,98304]{2,1,0:T(1,128)S(1)}, u32[]{:S(2)}, u32[]{:S(2)}) async-start(f32[8,1,98304]{2,1,0:T(1,128)} %reshape.50), calls=%async_computation | async-start | bytes 6291456 | tf_op jit(solution)/shard_map/all_to_all | solution.py:71
  156.2 4.0 %copy-start.5 = (s32[16,256]{1,0:T(8,128)S(1)}, s32[16,256]{1,0:T(8,128)}, u32[]{:S(2)}) copy-start(s32[16,256]{1,0:T(8,128)} %param.11) | copy-start | bytes 49156
  156.2 4.0 %copy-start.6 = (f32[16,256]{1,0:T(8,128)S(1)}, f32[16,256]{1,0:T(8,128)}, u32[]{:S(2)}) copy-start(f32[16,256]{1,0:T(8,128)} %param.13) | copy-start | bytes 49156
  156.2 4.0 %copy-start.7 = (f32[16,256]{1,0:T(8,128)S(1)}, f32[16,256]{1,0:T(8,128)}, u32[]{:S(2)}) copy-start(f32[16,256]{1,0:T(8,128)} %param.14) | copy-start | bytes 49156
  156.2 4.1 %copy-start.4 = (s32[16,256]{1,0:T(8,128)S(1)}, s32[16,256]{1,0:T(8,128)}, u32[]{:S(2)}) copy-start(s32[16,256]{1,0:T(8,128)} %param.12) | copy-start | bytes 49156
  156.2 41.8 %all-to-all-start.1 = ((f32[384,2,1024]{2,1,0:T(2,128)}), f32[384,2,1024]{2,1,0:T(2,128)S(1)}, u32[]{:S(2)}, u32[]{:S(2)}) async-start(f32[384,2,1024]{2,1,0:T(2,128)} %reshape_reshape.3), calls=%async_computation.1 | async-start | bytes 6291456 | tf_op jit(solution)/shard_map/all_to_all | solution.py:73
  217.3 10.7 %collective-permute-start = (f32[48,2,2,16,1]{0,3,4,2,1:T(8,128)S(1)}, f32[48,2,2,16,1]{0,3,4,2,1:T(8,128)S(1)}, u32[]{:S(2)}, u32[]{:S(2)}) collective-permute-start(f32[48,2,2,16,1]{0,3,4,2,1:T(8,128)S(1)} %copy.26), channel_id=1, source_target_pairs={{1,0},{2,1},{3,2},{5,4},{6,5},{7,6},{9,8},{10,9},{11,10},{13,12},{... | collective-permute-start | bytes 36872 | tf_op jit(solution)/shard_map/ppermute | solution.py:19
  220.8 9.6 %collective-permute-start.1 = (f32[48,2,2,16,1]{0,3,4,2,1:T(8,128)S(1)}, f32[48,2,2,16,1]{0,3,4,2,1:T(8,128)S(1)}, u32[]{:S(2)}, u32[]{:S(2)}) collective-permute-start(f32[48,2,2,16,1]{0,3,4,2,1:T(8,128)S(1)} %copy.28), channel_id=1, source_target_pairs={{0,1},{1,2},{2,3},{4,5},{5,6},{6,7},{8,9},{9,10},{10,11},{12,13},{... | collective-permute-start | bytes 36872 | tf_op jit(solution)/shard_map/ppermute | solution.py:18
  228.0 4.7 %copy-start.2 = (f32[48,2,2,16,255]{4,3,2,1,0:T(8,128)S(1)}, f32[48,2,2,16,255]{4,3,2,1,0:T(8,128)}, u32[]{:S(2)}) copy-start(f32[48,2,2,16,255]{4,3,2,1,0:T(8,128)} %get-tuple-element.73) | copy-start | bytes 9400324
  232.7 4.3 %copy-start = (f32[48,2,2,16,256]{4,3,2,1,0:T(8,128)S(1)}, f32[48,2,2,16,256]{4,3,2,1,0:T(8,128)}, u32[]{:S(2)}) copy-start(f32[48,2,2,16,256]{4,3,2,1,0:T(8,128)} %fusion.7) | copy-start | bytes 9437188
  232.7 4.7 %copy-start.1 = (f32[48,2,2,16,256]{4,3,2,1,0:T(8,128)S(1)}, f32[48,2,2,16,256]{4,3,2,1,0:T(8,128)}, u32[]{:S(2)}) copy-start(f32[48,2,2,16,256]{4,3,2,1,0:T(8,128)} %get-tuple-element.69) | copy-start | bytes 9437188
where the time goes:
time: 267 us; the launch traced here: 263 us
  local copies, waits for them, and re-layouts  90.8 us (34%)
  waiting for transfers between devices  74.5 us (28%)
  other arithmetic  29.2 us (11%)
  matrix products  24.2 us (9%)
  blocking collectives  22.3 us (8%)
  starting transfers between devices  15.4 us (6%)
  loops' own time  5.18 us (2%)
    all_to_all x1, waiting for transfers between devices, shards(): lax.all_to_all(series_mean, 'tm', split_axis=0, concat_axis=2, tiled=True)  37.7 us
    unnamed x19, local copies, waits for them, and re-layouts  37.3 us
    all_to_all x1, waiting for transfers between devices, shards(): lax.all_to_all(flat_cells, 'tm', split_axis=2, concat_axis=0, tiled=True)  36.8 us
    psum x1, blocking collectives, shards(): summed = lax.psum(jnp.sum(conversion, axis=0), 'tm')  22.3 us
    dot_general x8, matrix products, one_block(): jnp.dot(matrix, window, precision=lax.Precision.HIGHEST, preferred_elemen...  16.8 us
    another operation x3, local copies, waits for them, and re-layouts, shards(): stacked = jnp.stack([velocity_u, velocity_v], axis=1)  12.1 us
    all_to_all x1, other arithmetic, shards(): lax.all_to_all(flat_cells, 'tm', split_axis=2, concat_axis=0, tiled=True)  11.2 us
    all_to_all x3, local copies, waits for them, and re-layouts, shards(): lax.all_to_all(flat_cells, 'tm', split_axis=2, concat_axis=0, tiled=True)  9.91 us
  transfers between devices with their start and end apart: 4, of which 2 were waited for; matrix products, arithmetic and copies ran while one was open for 3% of the time, Pallas kernels for 0%

commit v1 on v0

--- a/solution.py
+++ b/solution.py
@@ -6,6 +6,29 @@
 HALF = 24
 SNAPS = 48
 cutoff_freq = 1.0 / 40.0
+
+
+def in_blocks(x, dim, count):
+    shape = x.shape
+    blocks = x.reshape(*shape[:dim], count, shape[dim] // count, *shape[dim + 1 :])
+    return jnp.moveaxis(blocks, dim, 0)
+
+
+def joined_along(pieces, dim):
+    shape = list(pieces.shape[1:])
+    shape[dim] *= pieces.shape[0]
+    return jnp.moveaxis(pieces, 0, dim).reshape(shape)
+
+
+def pairwise_exchange(shard, axis, split_dim, concat_dim):
+    length, index = (lax.axis_size(axis), lax.axis_index(axis))
+    blocks = in_blocks(shard, split_dim, length)
+    outs = [blocks[index]]
+    for step in range(1, length):
+        sent = blocks[index ^ step]
+        outs.append(lax.ppermute(sent, axis, [(i, i ^ step) for i in range(length)]))
+    blocks = jnp.stack(outs)[index ^ jnp.arange(length)]
+    return joined_along(blocks, concat_dim)
 
 
 def extended(x, sides, width):
@@ -67,9 +90,7 @@
     stacked = jnp.stack([velocity_u, velocity_v], axis=1)
     full_shape = stacked.shape
     flat_cells = stacked.reshape(block_len, 2, -1)
-    series_mean = filter_series(
-        lax.all_to_all(flat_cells, "tm", split_axis=2, concat_axis=0, tiled=True)
-    )
+    series_mean = filter_series(pairwise_exchange(flat_cells, "tm", 2, 0))
     mean_flat = lax.all_to_all(series_mean, "tm", split_axis=0, concat_axis=2, tiled=True)
     mean_flow = mean_flat.reshape(full_shape)
     eddies = stacked - mean_flow

time: 267 us -> 210 us (0.79)
  local copies, waits for them, and re-layouts: 90.8 us -> 60.9 us
  waiting for transfers between devices: 74.5 us -> 59.1 us
  other arithmetic: 29.2 us -> 15.9 us
  starting transfers between devices: 15.4 us -> 19.5 us
    all_to_all x1 -> x0, waiting for transfers between devices: 36.8 us -> none  [shards(): lax.all_to_all(flat_cells, 'tm', split_axis=2, concat_axis=0, tiled=True)]
    unnamed x19 -> x23, local copies, waits for them, and re-layouts: 37.3 us -> 14.6 us
    ppermute x0 -> x7, waiting for transfers between devices: none -> 21.4 us  [pairwise_exchange(): lax.ppermute(sent, axis, [(i, i ^ step) for i in range(length)])]
    all_to_all x1 -> x0, other arithmetic: 11.2 us -> none  [shards(): lax.all_to_all(flat_cells, 'tm', split_axis=2, concat_axis=0, tiled=True)]
    all_to_all x3 -> x0, local copies, waits for them, and re-layouts: 9.91 us -> none  [shards(): lax.all_to_all(flat_cells, 'tm', split_axis=2, concat_axis=0, tiled=True)]
    ppermute x0 -> x7, starting transfers between devices: none -> 9.24 us  [pairwise_exchange(): lax.ppermute(sent, axis, [(i, i ^ step) for i in range(length)])]
    all_to_all x1 -> x0, starting transfers between devices: 5.44 us -> none  [shards(): lax.all_to_all(flat_cells, 'tm', split_axis=2, concat_axis=0, tiled=True)]
    gather x0 -> x2, local copies, waits for them, and re-layouts: none -> 5.06 us  [pairwise_exchange(): blocks = jnp.stack(outs)[index ^ jnp.arange(length)]]
  transfers between devices with their start and end apart: 4 -> 10, of which waited for: 2 -> 4; matrix products, arithmetic and copies ran while one was open for 3% -> 9% of each run, Pallas kernels for 0% -> 0%
where the time goes in v1:
time: 210 us; the launch traced here: 208 us
  local copies, waits for them, and re-layouts  60.9 us (29%)
  waiting for transfers between devices  59.1 us (28%)
  matrix products  24.1 us (11%)
  blocking collectives  22.3 us (11%)
  starting transfers between devices  19.5 us (9%)
  other arithmetic  15.9 us (8%)
  loops' own time  5.28 us (3%)
    all_to_all x1, waiting for transfers between devices, shards(): lax.all_to_all(series_mean, 'tm', split_axis=0, concat_axis=2, tiled=True)  37.8 us
    psum x1, blocking collectives, shards(): summed = lax.psum(jnp.sum(conversion, axis=0), 'tm')  22.3 us
    ppermute x7, waiting for transfers between devices, pairwise_exchange(): lax.ppermute(sent, axis, [(i, i ^ step) for i in range(length)])  21.4 us
    dot_general x8, matrix products, one_block(): jnp.dot(matrix, window, precision=lax.Precision.HIGHEST, preferred_elemen...  16.7 us
    unnamed x23, local copies, waits for them, and re-layouts  14.6 us
    ppermute x7, starting transfers between devices, pairwise_exchange(): lax.ppermute(sent, axis, [(i, i ^ step) for i in range(length)])  9.24 us
    another operation x3, local copies, waits for them, and re-layouts, shards(): stacked = jnp.stack([velocity_u, velocity_v], axis=1)  7.73 us
    dot_general x8, matrix products, one_block(): jnp.dot(matrix, valid_part, precision=lax.Precision.HIGHEST, preferred_el...  7.47 us
  transfers between devices with their start and end apart: 10, of which 4 were waited for; matrix products, arithmetic and copies ran while one was open for 9% of the time, Pallas kernels for 0%

profile of v1, /device:TPU:0, one launch (start us, length us, event | category | flops | bytes accessed | tf_op | source)
XLA Modules:
  0.0 208.1 jit_solution(14855600303451213229)
XLA Ops:
  0.7 2.7 %stack.42 = f32[48,1,8,1024]{3,2,0,1:T(8,128)} reshape(f32[48,2,16,256]{3,2,1,0:T(8,128)} %param.9) | data formatting | bytes 3145728 | tf_op jit(solution)/shard_map/stack | solution.py:90
  3.4 2.3 %copy_dynamic-update-slice_fusion.1 = f32[48,2,8,1024]{3,0,1,2:T(8,128)S(1)} fusion(f32[48,1,8,1024]{3,2,0,1:T(8,128)} %stack.42), kind=kLoop, calls=%fused_computation.25 | loop fusion | bytes 3145728
  5.7 2.7 %stack.43 = f32[48,1,8,1024]{3,2,0,1:T(8,128)} reshape(f32[48,2,16,256]{3,2,1,0:T(8,128)} %param.10) | data formatting | bytes 3145728 | tf_op jit(solution)/shard_map/stack | solution.py:90
  8.4 2.3 %copy_dynamic-update-slice_fusion = f32[48,2,8,1024]{3,0,1,2:T(8,128)S(1)} fusion(f32[48,2,8,1024]{3,0,1,2:T(8,128)S(1)} %copy_dynamic-update-slice_fusion.1, f32[48,1,8,1024]{3,2,0,1:T(8,128)} %stack.43), kind=kLoop, calls=%fused_computation.24 | loop fusion | bytes 3145728 | tf_op jit(solution)/shard_map/stack | solution.py:90
  10.7 1.5 dynamic-slice_bitcast_fusion
  12.6 2.5 %collective-permute-start.1 = (f32[48,2,1024]{2,0,1:T(8,128)}, f32[48,2,1024]{2,0,1:T(8,128)}, u32[]{:S(2)}, u32[]{:S(2)}) collective-permute-start(f32[48,2,1024]{2,0,1:T(8,128)} %get-tuple-element.80), channel_id=1, source_target_pairs={{0,8},{4,12},{8,0},{12,4},{16,24},{20,28},{24,16},{28,20},{1,9},{5... | collective-permute-start | bytes 1179656 | tf_op jit(solution)/shard_map/ppermute | solution.py:29
  15.3 1.7 collective-permute-start.3
  17.0 0.7 fusion.42
  17.8 0.8 bitcast_dynamic-update-slice_fusion.7
  18.6 2.6 %collective-permute-start.5 = (f32[48,2,1024]{2,0,1:T(8,128)}, f32[48,2,1024]{2,0,1:T(8,128)S(1)}, u32[]{:S(2)}, u32[]{:S(2)}) collective-permute-start(f32[48,2,1024]{2,0,1:T(8,128)} %get-tuple-element.76), channel_id=1, source_target_pairs={{0,24},{4,28},{8,16},{12,20},{16,8},{20,12},{24,0},{28,4},{1,25},{... | collective-permute-start | bytes 1179656 | tf_op jit(solution)/shard_map/ppermute | solution.py:29
  21.1 1.8 bitcast_dynamic-update-slice_fusion.6
  22.9 2.5 %collective-permute-done.1 = f32[48,2,1024]{2,0,1:T(8,128)} collective-permute-done((f32[48,2,1024]{2,0,1:T(8,128)}, f32[48,2,1024]{2,0,1:T(8,128)}, u32[]{:S(2)}, u32[]{:S(2)}) %collective-permute-start.1) | collective-permute-done | bytes 393248 | tf_op jit(solution)/shard_map/ppermute | solution.py:29
  25.4 1.8 collective-permute-start.6
  27.2 1.8 bitcast_dynamic-update-slice_fusion.5
  29.0 4.5 %collective-permute-done.2 = f32[48,2,1024]{2,0,1:T(8,128)} collective-permute-done((f32[48,2,1024]{2,0,1:T(8,128)}, f32[48,2,1024]{2,0,1:T(8,128)}, u32[]{:S(2)}, u32[]{:S(2)}) %collective-permute-start.2) | collective-permute-done | bytes 393248 | tf_op jit(solution)/shard_map/ppermute | solution.py:29
  33.5 1.8 bitcast_dynamic-update-slice_fusion.4
  35.2 1.8 bitcast_dynamic-update-slice_fusion.3
  37.0 14.4 %collective-permute-done.4 = f32[48,2,1024]{2,0,1:T(8,128)} collective-permute-done((f32[48,2,1024]{2,0,1:T(8,128)}, f32[48,2,1024]{2,0,1:T(8,128)}, u32[]{:S(2)}, u32[]{:S(2)}) %collective-permute-start.4) | collective-permute-done | bytes 393248 | tf_op jit(solution)/shard_map/ppermute | solution.py:29
  51.4 1.8 bitcast_dynamic-update-slice_fusion.2
  53.2 0.8 bitcast_dynamic-update-slice_fusion.1
  54.0 0.8 bitcast_dynamic-update-slice_fusion
  54.8 2.6 %gather_fusion = f32[8,48,2,1024]{3,1,2,0:T(8,128)S(1)} fusion(f32[8,48,2,1024]{3,1,2,0:T(8,128)} %bitcast_dynamic-update-slice_fusion, s32[1024]{0:T(1024)S(1)} %pad_clamp_fusion), kind=kCustom, calls=%fused_computation | custom fusion | bytes 6291488 | tf_op jit(solution)/shard_map/gather | solution.py:30
  57.5 2.4 %copy.17 = f32[8,48,2,1024]{3,2,1,0:T(2,128)S(1)} copy(f32[8,48,2,1024]{3,1,2,0:T(8,128)S(1)} %gather_fusion) | data formatting | bytes 6291456 | tf_op jit(solution)/shard_map/gather | solution.py:30
  59.9 1.4 copy.24
  61.7 34.1 %while.11 = (s32[]{:T(128)}, f32[8,48,2048]{2,1,0:T(8,128)}, s32[8]{0:T(128)S(1)}, f32[432,2048]{1,0:T(8,128)S(1)}, f32[48,96]{1,0:T(8,128)}, /*index=5*/f32[432...) while((s32[]{:T(128)}, f32[8,48,2048]{2,1,0:T(8,128)}, s32[8]{0:T(128)S(1)}, ...), condition=%wide.region_1.3_spmd.clone, body=%wide.region_0.2_spmd.clone.sunk | while | flops 113399816 | bytes 1224551 | solution.py:70
  61.7 0.6 dynamic_slice.35
  63.0 0.9 convolution_bitcast_fusion.2
  63.9 2.1 %fusion.60 = f32[8,48,2048]{2,1,0:T(8,128)} fusion(f32[8,48,2048]{2,1,0:T(8,128)} %get-tuple-element.132, s32[]{:T(128)} %get-tuple-element.131, f32[48,96]{1,0:T(8,128)} %get-tuple-element.145, f32[432,2048]{1,0:T(8,128)S(1)} %get-tuple-element.144, s32[]{:T(128)S(6)} %select_n.193, f32[48]{0:T(128)S(1)} %convolution_bitcast_fusion.2), kind=kOutput, calls=%fused_computation.3.clone.1 | convolution fusion | flops 113344512 | bytes 1205252 | tf_op jit(solution)/shard_map/while/body/eval_jaxpr/dot_general | solution.py:62
  66.0 0.6 dynamic_slice.35
  67.2 0.9 convolution_bitcast_fusion.2
  68.2 2.1 fusion.60
  70.2 0.6 dynamic_slice.35
  71.5 0.9 convolution_bitcast_fusion.2
  72.4 2.1 %fusion.60 = f32[8,48,2048]{2,1,0:T(8,128)} fusion(f32[8,48,2048]{2,1,0:T(8,128)} %get-tuple-element.132, s32[]{:T(128)} %get-tuple-element.131, f32[48,96]{1,0:T(8,128)} %get-tuple-element.145, f32[432,2048]{1,0:T(8,128)S(1)} %get-tuple-element.144, s32[]{:T(128)S(6)} %select_n.193, f32[48]{0:T(128)S(1)} %convolution_bitcast_fusion.2), kind=kOutput, calls=%fused_computation.3.clone.1 | convolution fusion | flops 113344512 | bytes 1205252 | tf_op jit(solution)/shard_map/while/body/eval_jaxpr/dot_general | solution.py:62
  75.8 0.9 convolution_bitcast_fusion.2
  76.7 2.1 fusion.60
  80.0 0.9 convolution_bitcast_fusion.2
  80.9 2.1 %fusion.60 = f32[8,48,2048]{2,1,0:T(8,128)} fusion(f32[8,48,2048]{2,1,0:T(8,128)} %get-tuple-element.132, s32[]{:T(128)} %get-tuple-element.131, f32[48,96]{1,0:T(8,128)} %get-tuple-element.145, f32[432,2048]{1,0:T(8,128)S(1)} %get-tuple-element.144, s32[]{:T(128)S(6)} %select_n.193, f32[48]{0:T(128)S(1)} %convolution_bitcast_fusion.2), kind=kOutput, calls=%fused_computation.3.clone.1 | convolution fusion | flops 113344512 | bytes 1205252 | tf_op jit(solution)/shard_map/while/body/eval_jaxpr/dot_general | solution.py:62
  84.3 0.9 convolution_bitcast_fusion.2
  85.2 2.1 %fusion.60 = f32[8,48,2048]{2,1,0:T(8,128)} fusion(f32[8,48,2048]{2,1,0:T(8,128)} %get-tuple-element.132, s32[]{:T(128)} %get-tuple-element.131, f32[48,96]{1,0:T(8,128)} %get-tuple-element.145, f32[432,2048]{1,0:T(8,128)S(1)} %get-tuple-element.144, s32[]{:T(128)S(6)} %select_n.193, f32[48]{0:T(128)S(1)} %convolution_bitcast_fusion.2), kind=kOutput, calls=%fused_computation.3.clone.1 | convolution fusion | flops 113344512 | bytes 1205252 | tf_op jit(solution)/shard_map/while/body/eval_jaxpr/dot_general | solution.py:62
  88.5 0.9 convolution_bitcast_fusion.2
  89.5 2.1 %fusion.60 = f32[8,48,2048]{2,1,0:T(8,128)} fusion(f32[8,48,2048]{2,1,0:T(8,128)} %get-tuple-element.132, s32[]{:T(128)} %get-tuple-element.131, f32[48,96]{1,0:T(8,128)} %get-tuple-element.145, f32[432,2048]{1,0:T(8,128)S(1)} %get-tuple-element.144, s32[]{:T(128)S(6)} %select_n.193, f32[48]{0:T(128)S(1)} %convolution_bitcast_fusion.2), kind=kOutput, calls=%fused_computation.3.clone.1 | convolution fusion | flops 113344512 | bytes 1205252 | tf_op jit(solution)/shard_map/while/body/eval_jaxpr/dot_general | solution.py:62
  92.8 0.9 convolution_bitcast_fusion.2
  93.7 2.1 %fusion.60 = f32[8,48,2048]{2,1,0:T(8,128)} fusion(f32[8,48,2048]{2,1,0:T(8,128)} %get-tuple-element.132, s32[]{:T(128)} %get-tuple-element.131, f32[48,96]{1,0:T(8,128)} %get-tuple-element.145, f32[432,2048]{1,0:T(8,128)S(1)} %get-tuple-element.144, s32[]{:T(128)S(6)} %select_n.193, f32[48]{0:T(128)S(1)} %convolution_bitcast_fusion.2), kind=kOutput, calls=%fused_computation.3.clone.1 | convolution fusion | flops 113344512 | bytes 1205252 | tf_op jit(solution)/shard_map/while/body/eval_jaxpr/dot_general | solution.py:62
  95.8 5.6 %reshape_reshape.8 = f32[384,2,1024]{2,1,0:T(2,128)} reshape(f32[8,48,2048]{2,1,0:T(8,128)} %get-tuple-element.38) | data formatting | bytes 6291456 | tf_op jit(solution)/shard_map/reshape;reshape | solution.py:84
  101.5 4.3 %all-to-all-start = ((f32[384,2,1024]{2,1,0:T(2,128)}), f32[384,2,1024]{2,1,0:T(2,128)S(1)}, u32[]{:S(2)}, u32[]{:S(2)}) async-start(f32[384,2,1024]{2,1,0:T(2,128)} %reshape_reshape.8), calls=%async_computation | async-start | bytes 6291456 | tf_op jit(solution)/shard_map/all_to_all | solution.py:94
  105.8 37.8 %all-to-all-done = f32[384,2,1024]{2,1,0:T(2,128)S(1)} async-done(((f32[384,2,1024]{2,1,0:T(2,128)}), f32[384,2,1024]{2,1,0:T(2,128)S(1)}, u32[]{:S(2)}, u32[]{:S(2)}) %all-to-all-start) | async-done | bytes 3145760 | tf_op jit(solution)/shard_map/all_to_all | solution.py:94
  143.6 1.0 copy.18
  144.6 1.8 copy.19
  146.4 2.6 %reshape.72 = f32[48,2,2,16,256]{4,3,2,1,0:T(8,128)} reshape(f32[48,2,8,1024]{3,2,1,0:T(8,128)S(1)} %copy.19) | data formatting | bytes 6291456 | tf_op jit(solution)/shard_map/reshape | solution.py:95
  149.0 5.7 %maximum_subtract_fusion = (f32[48,2,2,16,256]{4,3,2,1,0:T(8,128)}, f32[48,2,2,16,256]{4,3,2,1,0:T(8,128)S(1)}) fusion(f32[48,2,2,16,256]{4,3,2,1,0:T(8,128)} %reshape.72, f32[48,1,2,16,256]{4,3,2,1,0:T(8,128)} %bitcast.81, f32[48,1,2,16,256]{4,3,2,1,0:T(8,128)} %bitcast.80, f32[2,16,256]{2,1,0:T(8,128)S(1)} %fusion.15), kind=kLoop, calls=%fused_computation.13 | loop fusion | flops 2359296 | bytes 12615680 | tf_op jit(solution)/shard_map/sub | solution.py:96
  154.7 3.7 %fusion.48 = (f32[48,2,2,16,255]{4,3,2,1,0:T(8,128)}, f32[48,2,2,16,255]{4,3,2,1,0:T(8,128)}) fusion(f32[48,2,2,16,256]{4,3,2,1,0:T(8,128)S(1)} %get-tuple-element.70), kind=kLoop, calls=%fused_computation.105 | loop fusion | bytes 12533760 | tf_op jit(solution)/shard_map/slice | solution.py:104
  158.4 2.3 %fusion.47 = (f32[48,2,2,16,1]{4,3,2,1,0:T(8,128)}, f32[48,2,2,16,1]{4,3,2,1,0:T(8,128)}) fusion(f32[48,2,2,16,256]{4,3,2,1,0:T(8,128)S(1)} %get-tuple-element.70), kind=kLoop, calls=%fused_computation.104 | loop fusion | bytes 49152 | tf_op jit(solution)/shard_map/slice | solution.py:99
  160.7 2.2 %copy.20 = f32[48,2,2,16,1]{0,3,4,2,1:T(8,128)S(1)} copy(f32[48,2,2,16,1]{4,3,2,1,0:T(8,128)} %get-tuple-element.72) | data formatting | bytes 24576 | tf_op jit(solution)/shard_map/slice | solution.py:99
  162.9 1.3 collective-permute-start.7
  164.2 2.2 %copy.22 = f32[48,2,2,16,1]{0,3,4,2,1:T(8,128)S(1)} copy(f32[48,2,2,16,1]{4,3,2,1,0:T(8,128)} %get-tuple-element.71) | data formatting | bytes 24576 | tf_op jit(solution)/shard_map/slice | solution.py:99
  166.4 4.8 %collective-permute-start.8 = (f32[48,2,2,16,1]{0,3,4,2,1:T(8,128)S(1)}, f32[48,2,2,16,1]{0,3,4,2,1:T(8,128)S(1)}, u32[]{:S(2)}, u32[]{:S(2)}) collective-permute-start(f32[48,2,2,16,1]{0,3,4,2,1:T(8,128)S(1)} %copy.22), channel_id=1, source_target_pairs={{0,1},{1,2},{2,3},{4,5},{5,6},{6,7},{8,9},{9,10},{10,11},{12,13},{... | collective-permute-start | bytes 36872 | tf_op jit(solution)/shard_map/ppermute | solution.py:41
  171.1 2.4 %fusion.7 = f32[48,2,2,16,256]{4,3,2,1,0:T(8,128)} fusion(f32[48,2,2,16,256]{4,3,2,1,0:T(8,128)S(1)} %get-tuple-element.70, f32[16,256]{1,0:T(8,128)S(1)} %broadcast_divide_fusion), kind=kLoop, calls=%fused_computation.12 | loop fusion | flops 1572864 | bytes 6307840 | tf_op jit(solution)/shard_map/mul | solution.py:107
  173.5 2.4 %copy.21 = f32[48,2,2,16,1]{4,3,2,1,0:T(8,128)} copy(f32[48,2,2,16,1]{0,3,4,2,1:T(8,128)S(1)} %collective-permute-done.7) | data formatting | bytes 24576 | tf_op jit(solution)/shard_map/ppermute | solution.py:42
  175.9 2.4 %copy.23 = f32[48,2,2,16,1]{4,3,2,1,0:T(8,128)} copy(f32[48,2,2,16,1]{0,3,4,2,1:T(8,128)S(1)} %collective-permute-done.8) | data formatting | bytes 24576 | tf_op jit(solution)/shard_map/ppermute | solution.py:41
  178.3 4.3 %fusion.8 = f32[48,2,2,16,256]{4,3,2,1,0:T(8,128)S(1)} fusion(f32[48,2,2,16,1]{4,3,2,1,0:T(8,128)} %copy.21, f32[48,2,2,16,255]{4,3,2,1,0:T(8,128)} %get-tuple-element.74, f32[48,2,2,16,255]{4,3,2,1,0:T(8,128)S(1)} %copy-done.2, f32[48,2,2,16,1]{4,3,2,1,0:T(8,128)} %copy.23, f32[16,256]{1,0:T(8,128)S(1)} %broadcast_divide_fusion.1), kind=kLoop, calls=%fused_computation.15 | loop fusion | flops 3145728 | bytes 9453568 | tf_op jit(solution)/shard_map/mul | solution.py:105
  183.0 2.1 %fusion.45 = (f32[2,16,256]{2,1,0:T(8,128)S(1)}, bf16[48,2,16,256]{3,2,1,0:T(8,128)(2,1)}) fusion(f32[48,2,2,16,256]{4,3,2,1,0:T(8,128)S(1)} %copy-done, f32[48,2,2,16,256]{4,3,2,1,0:T(8,128)S(1)} %fusion.8, f32[48,2,2,16,256]{4,3,2,1,0:T(8,128)S(1)} %copy-done.1, f32[2,16,256]{2,1,0:T(8,128)S(1)} %fusion.44), kind=kLoop, calls=%fused_computation.103 | loop fusion | flops 4710400 | bytes 10289152 | tf_op jit(solution)/shard_map/reduce_sum | solution.py:116
  185.2 22.3 %psum.7 = f32[2,16,256]{2,1,0:T(8,128)S(1)} all-reduce(f32[2,16,256]{2,1,0:T(8,128)S(1)} %get-tuple-element.67), channel_id=1, replica_groups=mesh['tm'=8,'tile'=4] {'tm'}, use_global_device_ids=true, to_apply=%region_3.5 | all-reduce | flops 8192 | bytes 65536 | tf_op jit(solution)/shard_map/psum | solution.py:116
  207.5 0.6 broadcast_multiply_fusion.1
  (40 shorter events, 4.5 us)
Async XLA Ops:
  12.2 6.4 %collective-permute-start = (f32[48,2,1024]{2,0,1:T(8,128)}, f32[48,2,1024]{2,0,1:T(8,128)}, u32[]{:S(2)}, u32[]{:S(2)}) collective-permute-start(f32[48,2,1024]{2,0,1:T(8,128)} %get-tuple-element.81), channel_id=1, source_target_pairs={{0,4},{4,0},{8,12},{12,8},{16,20},{20,16},{24,28},{28,24},{1,5},{5... | collective-permute-start | bytes 1179656 | tf_op jit(solution)/shard_map/ppermute | solution.py:29
  12.6 12.8 %collective-permute-start.1 = (f32[48,2,1024]{2,0,1:T(8,128)}, f32[48,2,1024]{2,0,1:T(8,128)}, u32[]{:S(2)}, u32[]{:S(2)}) collective-permute-start(f32[48,2,1024]{2,0,1:T(8,128)} %get-tuple-element.80), channel_id=1, source_target_pairs={{0,8},{4,12},{8,0},{12,4},{16,24},{20,28},{24,16},{28,20},{1,9},{5... | collective-permute-start | bytes 1179656 | tf_op jit(solution)/shard_map/ppermute | solution.py:29
  15.1 18.3 %collective-permute-start.2 = (f32[48,2,1024]{2,0,1:T(8,128)}, f32[48,2,1024]{2,0,1:T(8,128)}, u32[]{:S(2)}, u32[]{:S(2)}) collective-permute-start(f32[48,2,1024]{2,0,1:T(8,128)} %get-tuple-element.79), channel_id=1, source_target_pairs={{0,12},{4,8},{8,4},{12,0},{16,28},{20,24},{24,20},{28,16},{1,13},{... | collective-permute-start | bytes 1179656 | tf_op jit(solution)/shard_map/ppermute | solution.py:29
  15.3 20.0 %collective-permute-start.3 = (f32[48,2,1024]{2,0,1:T(8,128)}, f32[48,2,1024]{2,0,1:T(8,128)}, u32[]{:S(2)}, u32[]{:S(2)}) collective-permute-start(f32[48,2,1024]{2,0,1:T(8,128)} %get-tuple-element.78), channel_id=1, source_target_pairs={{0,16},{4,20},{8,24},{12,28},{16,0},{20,4},{24,8},{28,12},{1,17},{... | collective-permute-start | bytes 1179656 | tf_op jit(solution)/shard_map/ppermute | solution.py:29
  17.0 34.4 %collective-permute-start.4 = (f32[48,2,1024]{2,0,1:T(8,128)}, f32[48,2,1024]{2,0,1:T(8,128)}, u32[]{:S(2)}, u32[]{:S(2)}) collective-permute-start(f32[48,2,1024]{2,0,1:T(8,128)} %get-tuple-element.77), channel_id=1, source_target_pairs={{0,20},{4,16},{8,28},{12,24},{16,4},{20,0},{24,12},{28,8},{1,21},{... | collective-permute-start | bytes 1179656 | tf_op jit(solution)/shard_map/ppermute | solution.py:29
  18.6 34.6 %collective-permute-start.5 = (f32[48,2,1024]{2,0,1:T(8,128)}, f32[48,2,1024]{2,0,1:T(8,128)S(1)}, u32[]{:S(2)}, u32[]{:S(2)}) collective-permute-start(f32[48,2,1024]{2,0,1:T(8,128)} %get-tuple-element.76), channel_id=1, source_target_pairs={{0,24},{4,28},{8,16},{12,20},{16,8},{20,12},{24,0},{28,4},{1,25},{... | collective-permute-start | bytes 1179656 | tf_op jit(solution)/shard_map/ppermute | solution.py:29
  25.4 28.6 %collective-permute-start.6 = (f32[48,2,1024]{2,0,1:T(8,128)S(1)}, f32[48,2,1024]{2,0,1:T(8,128)S(1)}, u32[]{:S(2)}, u32[]{:S(2)}) collective-permute-start(f32[48,2,1024]{2,0,1:T(8,128)S(1)} %get-tuple-element.75), channel_id=1, source_target_pairs={{0,28},{4,24},{8,20},{12,16},{16,12},{20,8},{24,4},{28,0},{1,29},{... | collective-permute-start | bytes 1179656 | tf_op jit(solution)/shard_map/ppermute | solution.py:29
  101.4 4.3 %copy-start.4 = (s32[16,256]{1,0:T(8,128)S(1)}, s32[16,256]{1,0:T(8,128)}, u32[]{:S(2)}) copy-start(s32[16,256]{1,0:T(8,128)} %param.11) | copy-start | bytes 49156
  101.4 4.3 %copy-start.5 = (f32[16,256]{1,0:T(8,128)S(1)}, f32[16,256]{1,0:T(8,128)}, u32[]{:S(2)}) copy-start(f32[16,256]{1,0:T(8,128)} %param.13) | copy-start | bytes 49156
  101.4 4.3 %copy-start.6 = (f32[16,256]{1,0:T(8,128)S(1)}, f32[16,256]{1,0:T(8,128)}, u32[]{:S(2)}) copy-start(f32[16,256]{1,0:T(8,128)} %param.14) | copy-start | bytes 49156
  101.4 4.3 %copy-start.3 = (s32[16,256]{1,0:T(8,128)S(1)}, s32[16,256]{1,0:T(8,128)}, u32[]{:S(2)}) copy-start(s32[16,256]{1,0:T(8,128)} %param.12) | copy-start | bytes 49156
  101.5 42.1 %all-to-all-start = ((f32[384,2,1024]{2,1,0:T(2,128)}), f32[384,2,1024]{2,1,0:T(2,128)S(1)}, u32[]{:S(2)}, u32[]{:S(2)}) async-start(f32[384,2,1024]{2,1,0:T(2,128)} %reshape_reshape.8), calls=%async_computation | async-start | bytes 6291456 | tf_op jit(solution)/shard_map/all_to_all | solution.py:94
  162.9 10.7 %collective-permute-start.7 = (f32[48,2,2,16,1]{0,3,4,2,1:T(8,128)S(1)}, f32[48,2,2,16,1]{0,3,4,2,1:T(8,128)S(1)}, u32[]{:S(2)}, u32[]{:S(2)}) collective-permute-start(f32[48,2,2,16,1]{0,3,4,2,1:T(8,128)S(1)} %copy.20), channel_id=1, source_target_pairs={{1,0},{2,1},{3,2},{5,4},{6,5},{7,6},{9,8},{10,9},{11,10},{13,12},{... | collective-permute-start | bytes 36872 | tf_op jit(solution)/shard_map/ppermute | solution.py:42
  166.4 9.6 %collective-permute-start.8 = (f32[48,2,2,16,1]{0,3,4,2,1:T(8,128)S(1)}, f32[48,2,2,16,1]{0,3,4,2,1:T(8,128)S(1)}, u32[]{:S(2)}, u32[]{:S(2)}) collective-permute-start(f32[48,2,2,16,1]{0,3,4,2,1:T(8,128)S(1)} %copy.22), channel_id=1, source_target_pairs={{0,1},{1,2},{2,3},{4,5},{5,6},{6,7},{8,9},{9,10},{10,11},{12,13},{... | collective-permute-start | bytes 36872 | tf_op jit(solution)/shard_map/ppermute | solution.py:41
  173.5 4.8 %copy-start.2 = (f32[48,2,2,16,255]{4,3,2,1,0:T(8,128)S(1)}, f32[48,2,2,16,255]{4,3,2,1,0:T(8,128)}, u32[]{:S(2)}) copy-start(f32[48,2,2,16,255]{4,3,2,1,0:T(8,128)} %get-tuple-element.73) | copy-start | bytes 9400324
  178.3 4.3 %copy-start = (f32[48,2,2,16,256]{4,3,2,1,0:T(8,128)S(1)}, f32[48,2,2,16,256]{4,3,2,1,0:T(8,128)}, u32[]{:S(2)}) copy-start(f32[48,2,2,16,256]{4,3,2,1,0:T(8,128)} %fusion.7) | copy-start | bytes 9437188
  178.3 4.7 %copy-start.1 = (f32[48,2,2,16,256]{4,3,2,1,0:T(8,128)S(1)}, f32[48,2,2,16,256]{4,3,2,1,0:T(8,128)}, u32[]{:S(2)}) copy-start(f32[48,2,2,16,256]{4,3,2,1,0:T(8,128)} %get-tuple-element.69) | copy-start | bytes 9437188
